TPU v7x, 512 devices: a whole 4x8x8 slice. The times are simulated.
512 devices in a mesh: ctx: 64 (over x, z, core), head: 8 (over y).
Axes of the slice: x: 4, y: 8, z: 8, core: 2. Of those that a mesh axis runs over, the one named last changes fastest.
Arguments:
- queries: bfloat16 [32768, 4096], P('ctx', 'head'), may hold values from -6 to 6
- keys: bfloat16 [32768, 4096], P('ctx', 'head'), may hold values from -6 to 6
- values: bfloat16 [32768, 4096], P('ctx', 'head'), may hold values from -6 to 6
- out_grad: bfloat16 [32768, 4096], P(('ctx', 'head')), may hold values from -6 to 6
Outputs:
- query_grad: bfloat16 [32768, 4096], P('ctx', 'head')
- key_grad: bfloat16 [32768, 4096], P('ctx', 'head')
- value_grad: bfloat16 [32768, 4096], P('ctx', 'head')
All inputs are finite; a program needn't handle non-finite values.
Results may differ from a plain program's by a relative error of at most 0.0049.
Values may be sent and summed in bfloat16 or wider, within the bound.
A program may use at most 128 MiB of HBM per device.

v0:
```python
import math

import jax
import jax.numpy as jnp
from jax import lax
from jax.sharding import PartitionSpec as P

HEAD_DIM = 128


def from_behind(x, axis, by):
    length = lax.axis_size(axis)
    pairs = [(i, i + by) for i in range(length) if 0 <= i + by < length]
    return lax.ppermute(x, axis, pairs)


def forward_prefix(own_term, device_count):
    running = own_term
    reach = 1
    while reach < device_count:
        running = running + from_behind(running, "ctx", reach)
        reach = reach * 2
    return running - own_term


def backward_prefix(own_term, device_count):
    running = own_term
    reach = 1
    while reach < device_count:
        running = running + from_behind(running, "ctx", -reach)
        reach = reach * 2
    return running - own_term


def local(queries, keys, values, out_grad):
    row_count = queries.shape[0]
    heads_here = queries.shape[1] // HEAD_DIM
    grad_flat = lax.all_to_all(out_grad, "head", split_axis=1, concat_axis=0, tiled=True)
    device_count = lax.axis_size("ctx")
    factor = 1.0 / math.sqrt(HEAD_DIM * row_count * device_count)
    shaped = (row_count, heads_here, HEAD_DIM)
    query_rows = queries.reshape(shaped)
    key_rows = keys.reshape(shaped)
    value_rows = values.reshape(shaped)
    grad_rows = grad_flat.reshape(shaped)
    key_values = jnp.einsum(
        "thd,the->hde", key_rows, value_rows, preferred_element_type=jnp.float32
    )
    query_grads = jnp.einsum(
        "thd,the->hde", query_rows, grad_rows, preferred_element_type=jnp.float32
    )
    before = forward_prefix(key_values, device_count)
    after = backward_prefix(query_grads, device_count)
    key_state = before.astype(jnp.bfloat16)
    grad_state = after.astype(jnp.bfloat16)
    causal = jnp.tril(jnp.ones((row_count, row_count), jnp.bool_))
    scores = jnp.einsum("ihd,jhd->hij", query_rows, key_rows, preferred_element_type=jnp.float32)
    attend = jnp.where(causal[None], scores, 0.0).astype(jnp.bfloat16)
    mixed = jnp.einsum("ihe,jhe->hij", grad_rows, value_rows, preferred_element_type=jnp.float32)
    upstream = jnp.where(causal[None], mixed, 0.0).astype(jnp.bfloat16)
    query_out = jnp.einsum(
        "hij,jhd->ihd", upstream, key_rows, preferred_element_type=jnp.float32
    ) + jnp.einsum("ihe,hde->ihd", grad_rows, key_state, preferred_element_type=jnp.float32)
    key_out = jnp.einsum(
        "hij,ihd->jhd", upstream, query_rows, preferred_element_type=jnp.float32
    ) + jnp.einsum("jhe,hde->jhd", value_rows, grad_state, preferred_element_type=jnp.float32)
    value_out = jnp.einsum(
        "hij,ihe->jhe", attend, grad_rows, preferred_element_type=jnp.float32
    ) + jnp.einsum("jhd,hde->jhe", key_rows, grad_state, preferred_element_type=jnp.float32)
    flat = (row_count, heads_here * HEAD_DIM)
    return (
        (query_out * factor).astype(jnp.bfloat16).reshape(flat),
        (key_out * factor).astype(jnp.bfloat16).reshape(flat),
        (value_out * factor).astype(jnp.bfloat16).reshape(flat),
    )


def solution(mesh):
    return jax.shard_map(
        local,
        mesh=mesh,
        in_specs=(P("ctx", "head"), P("ctx", "head"), P("ctx", "head"), P(("ctx", "head"), None)),
        out_specs=(P("ctx", "head"), P("ctx", "head"), P("ctx", "head")),
        check_vma=False,
    )
```

profile of v0, /device:TPU:72, one launch (start us, length us, event | category | flops | bytes accessed | tf_op | source)
XLA Modules:
  0.0 135.2 jit_solution(8368806050284982367)
XLA Ops:
  0.7 2.0 %copy.86 = bf16[8,8,8,512]{3,2,0,1:T(8,128)(2,1)} copy(bf16[8,8,8,512]{3,2,1,0:T(8,128)(2,1)} %bitcast.110) | data formatting | bytes 1048576 | tf_op jit(solution)/shard_map/all_to_all | solution.py:38
  2.6 7.5 %all-to-all-start = ((bf16[64,8,512]{2,0,1:T(8,128)(2,1)}), bf16[64,8,512]{2,0,1:T(8,128)(2,1)S(1)}, u32[]{:S(2)}, u32[]{:S(2)}) async-start(bf16[64,8,512]{2,0,1:T(8,128)(2,1)} %bitcast.105), calls=%async_computation | async-start | bytes 1048576 | tf_op jit(solution)/shard_map/all_to_all | solution.py:38
  10.6 2.1 %collective-permute-start = (f32[4,128,128]{2,1,0:T(8,128)S(1)}, f32[4,128,128]{2,1,0:T(8,128)S(1)}, u32[]{:S(2)}, u32[]{:S(2)}) collective-permute-start(f32[4,128,128]{2,1,0:T(8,128)S(1)} %fusion.18), channel_id=1, source_target_pairs={{0,8},{8,16},{16,24},{24,32},{32,40},{40,48},{48,56},{56,64},{64,7... | collective-permute-start | bytes 786440 | tf_op jit(solution)/shard_map/ppermute | solution.py:14
  12.6 5.8 %collective-permute-done = f32[4,128,128]{2,1,0:T(8,128)S(1)} collective-permute-done((f32[4,128,128]{2,1,0:T(8,128)S(1)}, f32[4,128,128]{2,1,0:T(8,128)S(1)}, u32[]{:S(2)}, u32[]{:S(2)}) %collective-permute-start) | collective-permute-done | bytes 262176 | tf_op jit(solution)/shard_map/ppermute | solution.py:14
  18.4 4.3 %collective-permute-start.1 = (f32[4,128,128]{2,1,0:T(8,128)S(1)}, f32[4,128,128]{2,1,0:T(8,128)S(1)}, u32[]{:S(2)}, u32[]{:S(2)}) collective-permute-start(f32[4,128,128]{2,1,0:T(8,128)S(1)} %add.45), channel_id=1, source_target_pairs={{0,16},{8,24},{16,32},{24,40},{32,48},{40,56},{48,64},{56,72},{64,... | collective-permute-start | bytes 786440 | tf_op jit(solution)/shard_map/ppermute | solution.py:14
  22.7 5.8 %collective-permute-done.1 = f32[4,128,128]{2,1,0:T(8,128)S(1)} collective-permute-done((f32[4,128,128]{2,1,0:T(8,128)S(1)}, f32[4,128,128]{2,1,0:T(8,128)S(1)}, u32[]{:S(2)}, u32[]{:S(2)}) %collective-permute-start.1) | collective-permute-done | bytes 262176 | tf_op jit(solution)/shard_map/ppermute | solution.py:14
  29.3 7.5 %collective-permute-start.2 = (f32[4,128,128]{2,1,0:T(8,128)}, f32[4,128,128]{2,1,0:T(8,128)}, u32[]{:S(2)}, u32[]{:S(2)}) collective-permute-start(f32[4,128,128]{2,1,0:T(8,128)} %add.46), channel_id=1, source_target_pairs={{0,32},{8,40},{16,48},{24,56},{32,64},{40,72},{48,80},{56,88},{64,... | collective-permute-start | bytes 786440 | tf_op jit(solution)/shard_map/ppermute | solution.py:14
  37.6 1.9 %collective-permute-start.6 = (f32[4,128,128]{2,1,0:T(8,128)S(1)}, f32[4,128,128]{2,1,0:T(8,128)S(1)}, u32[]{:S(2)}, u32[]{:S(2)}) collective-permute-start(f32[4,128,128]{2,1,0:T(8,128)S(1)} %fusion.11), channel_id=1, source_target_pairs={{8,0},{16,8},{24,16},{32,24},{40,32},{48,40},{56,48},{64,56},{72,6... | collective-permute-start | bytes 786440 | tf_op jit(solution)/shard_map/ppermute | solution.py:14
  39.6 8.2 %collective-permute-done.2 = f32[4,128,128]{2,1,0:T(8,128)} collective-permute-done((f32[4,128,128]{2,1,0:T(8,128)}, f32[4,128,128]{2,1,0:T(8,128)}, u32[]{:S(2)}, u32[]{:S(2)}) %collective-permute-start.2) | collective-permute-done | bytes 262176 | tf_op jit(solution)/shard_map/ppermute | solution.py:14
  48.8 7.0 %collective-permute-start.3 = (f32[4,128,128]{2,1,0:T(8,128)S(1)}, f32[4,128,128]{2,1,0:T(8,128)S(1)}, u32[]{:S(2)}, u32[]{:S(2)}) collective-permute-start(f32[4,128,128]{2,1,0:T(8,128)S(1)} %add.47), channel_id=1, source_target_pairs={{0,64},{8,72},{16,80},{24,88},{32,96},{40,104},{48,112},{56,120},{... | collective-permute-start | bytes 786440 | tf_op jit(solution)/shard_map/ppermute | solution.py:14
  55.8 1.9 %collective-permute-start.7 = (f32[4,128,128]{2,1,0:T(8,128)S(1)}, f32[4,128,128]{2,1,0:T(8,128)S(1)}, u32[]{:S(2)}, u32[]{:S(2)}) collective-permute-start(f32[4,128,128]{2,1,0:T(8,128)S(1)} %add.52), channel_id=1, source_target_pairs={{16,0},{24,8},{32,16},{40,24},{48,32},{56,40},{64,48},{72,56},{80,... | collective-permute-start | bytes 786440 | tf_op jit(solution)/shard_map/ppermute | solution.py:14
  58.6 12.1 %collective-permute-done.7 = f32[4,128,128]{2,1,0:T(8,128)S(1)} collective-permute-done((f32[4,128,128]{2,1,0:T(8,128)S(1)}, f32[4,128,128]{2,1,0:T(8,128)S(1)}, u32[]{:S(2)}, u32[]{:S(2)}) %collective-permute-start.7) | collective-permute-done | bytes 262176 | tf_op jit(solution)/shard_map/ppermute | solution.py:14
  70.7 1.4 %collective-permute-start.8 = (f32[4,128,128]{2,1,0:T(8,128)S(1)}, f32[4,128,128]{2,1,0:T(8,128)S(1)}, u32[]{:S(2)}, u32[]{:S(2)}) collective-permute-start(f32[4,128,128]{2,1,0:T(8,128)S(1)} %add.53), channel_id=1, source_target_pairs={{32,0},{40,8},{48,16},{56,24},{64,32},{72,40},{80,48},{88,56},{96,... | collective-permute-start | bytes 786440 | tf_op jit(solution)/shard_map/ppermute | solution.py:14
  73.1 8.9 %collective-permute-start.4 = (f32[4,128,128]{2,1,0:T(8,128)S(1)}, f32[4,128,128]{2,1,0:T(8,128)S(1)}, u32[]{:S(2)}, u32[]{:S(2)}) collective-permute-start(f32[4,128,128]{2,1,0:T(8,128)S(1)} %add.48), channel_id=1, source_target_pairs={{0,128},{8,136},{16,144},{24,152},{32,160},{40,168},{48,176},{56,1... | collective-permute-start | bytes 786440 | tf_op jit(solution)/shard_map/ppermute | solution.py:14
  82.0 5.9 %collective-permute-done.8 = f32[4,128,128]{2,1,0:T(8,128)S(1)} collective-permute-done((f32[4,128,128]{2,1,0:T(8,128)S(1)}, f32[4,128,128]{2,1,0:T(8,128)S(1)}, u32[]{:S(2)}, u32[]{:S(2)}) %collective-permute-start.8) | collective-permute-done | bytes 262176 | tf_op jit(solution)/shard_map/ppermute | solution.py:14
  90.5 11.6 %collective-permute-start.5 = (f32[4,128,128]{2,1,0:T(8,128)}, f32[4,128,128]{2,1,0:T(8,128)}, u32[]{:S(2)}, u32[]{:S(2)}) collective-permute-start(f32[4,128,128]{2,1,0:T(8,128)} %add.49), channel_id=1, source_target_pairs={{0,256},{8,264},{16,272},{24,280},{32,288},{40,296},{48,304},{56,3... | collective-permute-start | bytes 786440 | tf_op jit(solution)/shard_map/ppermute | solution.py:14
  102.1 5.5 %collective-permute-done.9 = f32[4,128,128]{2,1,0:T(8,128)S(1)} collective-permute-done((f32[4,128,128]{2,1,0:T(8,128)S(1)}, f32[4,128,128]{2,1,0:T(8,128)S(1)}, u32[]{:S(2)}, u32[]{:S(2)}) %collective-permute-start.9) | collective-permute-done | bytes 262176 | tf_op jit(solution)/shard_map/ppermute | solution.py:14
  109.6 3.3 %fusion.1 = f32[512,4,128]{0,2,1:T(8,128)} fusion(bf16[512,4,128]{0,2,1:T(8,128)(2,1)S(1)} %copy.31, pred[512,512]{1,0:T(8,128)(4,1)} %copy-done.6, bf16[512,512]{1,0:T(8,128)(2,1)} %param.4, bf16[512,512]{1,0:T(8,128)(2,1)} %param.5), kind=kOutput, calls=%fused_computation.5 | convolution fusion | flops 538968064 | bytes 2883584 | tf_op jit(solution)/shard_map/hij,ihe->jhe/dot_general | solution.py:67
  112.9 5.2 %collective-permute-done.10 = f32[4,128,128]{2,1,0:T(8,128)} collective-permute-done((f32[4,128,128]{2,1,0:T(8,128)}, f32[4,128,128]{2,1,0:T(8,128)}, u32[]{:S(2)}, u32[]{:S(2)}) %collective-permute-start.10) | collective-permute-done | bytes 262176 | tf_op jit(solution)/shard_map/ppermute | solution.py:14
  118.1 1.8 %add.56 = f32[4,128,128]{2,1,0:T(8,128)} add(f32[4,128,128]{2,1,0:T(8,128)} %add.55, f32[4,128,128]{2,1,0:T(8,128)} %collective-permute-done.10) | non-fusion elementwise | flops 65536 | bytes 786432 | tf_op jit(solution)/shard_map/add | solution.py:30
  121.2 2.2 %fusion.8 = bf16[512,4,128]{0,2,1:T(8,128)(2,1)} fusion(f32[512,4,128]{0,2,1:T(8,128)S(1)} %convolution_bitcast_fusion.1, bf16[512,4,128]{0,2,1:T(8,128)(2,1)S(1)} %copy.31, f32[4,128,128]{2,1,0:T(8,128)} %copy-done.5, f32[4,128,128]{2,1,0:T(8,128)} %add.49, f32[4,128,128]{2,1,0:T(8,128)} %collective-permute-done.5), kind=kOutput, calls=%fused_computation.15 | convolution fusion | flops 68091904 | bytes 2883584 | tf_op jit(solution)/shard_map/ihe,hde->ihd/dot_general | solution.py:63
  123.4 2.0 %copy.34 = bf16[512,512]{1,0:T(8,128)(2,1)} copy(bf16[512,512]{0,1:T(8,128)(2,1)} %bitcast.109) | data formatting | bytes 1048576
  125.4 4.8 %collective-permute-done.11 = f32[4,128,128]{2,1,0:T(8,128)} collective-permute-done((f32[4,128,128]{2,1,0:T(8,128)}, f32[4,128,128]{2,1,0:T(8,128)}, u32[]{:S(2)}, u32[]{:S(2)}) %collective-permute-start.11) | collective-permute-done | bytes 262176 | tf_op jit(solution)/shard_map/ppermute | solution.py:14
  132.7 1.6 %fusion.10 = bf16[512,4,128]{0,2,1:T(8,128)(2,1)S(1)} fusion(f32[512,4,128]{0,2,1:T(8,128)} %fusion.1, bf16[4,128,128]{2,1,0:T(8,128)(2,1)S(1)} %subtract_convert_fusion, bf16[512,512]{1,0:T(8,128)(2,1)S(1)} %copy-done.2), kind=kOutput, calls=%fused_computation.17 | convolution fusion | flops 67895296 | bytes 2228224 | tf_op jit(solution)/shard_map/jhd,hde->jhe/dot_general | solution.py:69
  (43 shorter events, 14.1 us)
Async XLA Ops:
  0.6 9.5 %copy-start = (bf16[512,512]{1,0:T(8,128)(2,1)S(1)}, bf16[512,512]{1,0:T(8,128)(2,1)}, u32[]{:S(2)}) copy-start(bf16[512,512]{1,0:T(8,128)(2,1)} %param.6) | copy-start | bytes 1572868
  0.6 9.5 %copy-start.1 = (bf16[512,512]{1,0:T(8,128)(2,1)S(1)}, bf16[512,512]{1,0:T(8,128)(2,1)}, u32[]{:S(2)}) copy-start(bf16[512,512]{1,0:T(8,128)(2,1)} %param.5) | copy-start | bytes 1572868
  2.6 34.1 %all-to-all-start = ((bf16[64,8,512]{2,0,1:T(8,128)(2,1)}), bf16[64,8,512]{2,0,1:T(8,128)(2,1)S(1)}, u32[]{:S(2)}, u32[]{:S(2)}) async-start(bf16[64,8,512]{2,0,1:T(8,128)(2,1)} %bitcast.105), calls=%async_computation | async-start | bytes 1048576 | tf_op jit(solution)/shard_map/all_to_all | solution.py:38
  10.5 26.2 %copy-start.5 = (f32[4,128,128]{2,1,0:T(8,128)}, f32[4,128,128]{2,1,0:T(8,128)S(1)}, u32[]{:S(2)}) copy-start(f32[4,128,128]{2,1,0:T(8,128)S(1)} %fusion.18) | copy-start | bytes 786436
  10.5 26.7 %copy-start.3 = (bf16[512,512]{1,0:T(8,128)(2,1)S(1)}, bf16[512,512]{1,0:T(8,128)(2,1)}, u32[]{:S(2)}) copy-start(bf16[512,512]{1,0:T(8,128)(2,1)} %param.4) | copy-start | bytes 1572868
  10.6 7.8 %collective-permute-start = (f32[4,128,128]{2,1,0:T(8,128)S(1)}, f32[4,128,128]{2,1,0:T(8,128)S(1)}, u32[]{:S(2)}, u32[]{:S(2)}) collective-permute-start(f32[4,128,128]{2,1,0:T(8,128)S(1)} %fusion.18), channel_id=1, source_target_pairs={{0,8},{8,16},{16,24},{24,32},{32,40},{40,48},{48,56},{56,64},{64,7... | collective-permute-start | bytes 786440 | tf_op jit(solution)/shard_map/ppermute | solution.py:14
  18.4 10.1 %collective-permute-start.1 = (f32[4,128,128]{2,1,0:T(8,128)S(1)}, f32[4,128,128]{2,1,0:T(8,128)S(1)}, u32[]{:S(2)}, u32[]{:S(2)}) collective-permute-start(f32[4,128,128]{2,1,0:T(8,128)S(1)} %add.45), channel_id=1, source_target_pairs={{0,16},{8,24},{16,32},{24,40},{32,48},{40,56},{48,64},{56,72},{64,... | collective-permute-start | bytes 786440 | tf_op jit(solution)/shard_map/ppermute | solution.py:14
  29.3 18.5 %collective-permute-start.2 = (f32[4,128,128]{2,1,0:T(8,128)}, f32[4,128,128]{2,1,0:T(8,128)}, u32[]{:S(2)}, u32[]{:S(2)}) collective-permute-start(f32[4,128,128]{2,1,0:T(8,128)} %add.46), channel_id=1, source_target_pairs={{0,32},{8,40},{16,48},{24,56},{32,64},{40,72},{48,80},{56,88},{64,... | collective-permute-start | bytes 786440 | tf_op jit(solution)/shard_map/ppermute | solution.py:14
  37.6 18.2 %collective-permute-start.6 = (f32[4,128,128]{2,1,0:T(8,128)S(1)}, f32[4,128,128]{2,1,0:T(8,128)S(1)}, u32[]{:S(2)}, u32[]{:S(2)}) collective-permute-start(f32[4,128,128]{2,1,0:T(8,128)S(1)} %fusion.11), channel_id=1, source_target_pairs={{8,0},{16,8},{24,16},{32,24},{40,32},{48,40},{56,48},{64,56},{72,6... | collective-permute-start | bytes 786440 | tf_op jit(solution)/shard_map/ppermute | solution.py:14
  39.6 19.0 %copy-start.6 = (pred[512,512]{1,0:T(8,128)(4,1)}, pred[512,512]{1,0:T(8,128)(4,1)S(1)}, u32[]{:S(2)}) copy-start(pred[512,512]{1,0:T(8,128)(4,1)S(1)} %iota_compare_fusion) | copy-start | bytes 786436
  48.8 24.2 %collective-permute-start.3 = (f32[4,128,128]{2,1,0:T(8,128)S(1)}, f32[4,128,128]{2,1,0:T(8,128)S(1)}, u32[]{:S(2)}, u32[]{:S(2)}) collective-permute-start(f32[4,128,128]{2,1,0:T(8,128)S(1)} %add.47), channel_id=1, source_target_pairs={{0,64},{8,72},{16,80},{24,88},{32,96},{40,104},{48,112},{56,120},{... | collective-permute-start | bytes 786440 | tf_op jit(solution)/shard_map/ppermute | solution.py:14
  55.8 14.9 %collective-permute-start.7 = (f32[4,128,128]{2,1,0:T(8,128)S(1)}, f32[4,128,128]{2,1,0:T(8,128)S(1)}, u32[]{:S(2)}, u32[]{:S(2)}) collective-permute-start(f32[4,128,128]{2,1,0:T(8,128)S(1)} %add.52), channel_id=1, source_target_pairs={{16,0},{24,8},{32,16},{40,24},{48,32},{56,40},{64,48},{72,56},{80,... | collective-permute-start | bytes 786440 | tf_op jit(solution)/shard_map/ppermute | solution.py:14
  70.7 18.5 %copy-start.4 = (bf16[512,512]{1,0:T(8,128)(2,1)S(1)}, bf16[512,512]{1,0:T(8,128)(2,1)}, u32[]{:S(2)}) copy-start(bf16[512,512]{1,0:T(8,128)(2,1)} %param.4) | copy-start | bytes 1572868
  70.7 17.1 %collective-permute-start.8 = (f32[4,128,128]{2,1,0:T(8,128)S(1)}, f32[4,128,128]{2,1,0:T(8,128)S(1)}, u32[]{:S(2)}, u32[]{:S(2)}) collective-permute-start(f32[4,128,128]{2,1,0:T(8,128)S(1)} %add.53), channel_id=1, source_target_pairs={{32,0},{40,8},{48,16},{56,24},{64,32},{72,40},{80,48},{88,56},{96,... | collective-permute-start | bytes 786440 | tf_op jit(solution)/shard_map/ppermute | solution.py:14
  73.1 16.7 %collective-permute-start.4 = (f32[4,128,128]{2,1,0:T(8,128)S(1)}, f32[4,128,128]{2,1,0:T(8,128)S(1)}, u32[]{:S(2)}, u32[]{:S(2)}) collective-permute-start(f32[4,128,128]{2,1,0:T(8,128)S(1)} %add.48), channel_id=1, source_target_pairs={{0,128},{8,136},{16,144},{24,152},{32,160},{40,168},{48,176},{56,1... | collective-permute-start | bytes 786440 | tf_op jit(solution)/shard_map/ppermute | solution.py:14
  87.9 19.7 %collective-permute-start.9 = (f32[4,128,128]{2,1,0:T(8,128)S(1)}, f32[4,128,128]{2,1,0:T(8,128)S(1)}, u32[]{:S(2)}, u32[]{:S(2)}) collective-permute-start(f32[4,128,128]{2,1,0:T(8,128)S(1)} %add.54), channel_id=1, source_target_pairs={{64,0},{72,8},{80,16},{88,24},{96,32},{104,40},{112,48},{120,56},{... | collective-permute-start | bytes 786440 | tf_op jit(solution)/shard_map/ppermute | solution.py:14
  90.5 30.7 %collective-permute-start.5 = (f32[4,128,128]{2,1,0:T(8,128)}, f32[4,128,128]{2,1,0:T(8,128)}, u32[]{:S(2)}, u32[]{:S(2)}) collective-permute-start(f32[4,128,128]{2,1,0:T(8,128)} %add.49), channel_id=1, source_target_pairs={{0,256},{8,264},{16,272},{24,280},{32,288},{40,296},{48,304},{56,3... | collective-permute-start | bytes 786440 | tf_op jit(solution)/shard_map/ppermute | solution.py:14
  108.3 9.8 %collective-permute-start.10 = (f32[4,128,128]{2,1,0:T(8,128)}, f32[4,128,128]{2,1,0:T(8,128)}, u32[]{:S(2)}, u32[]{:S(2)}) collective-permute-start(f32[4,128,128]{2,1,0:T(8,128)} %add.55), channel_id=1, source_target_pairs={{128,0},{136,8},{144,16},{152,24},{160,32},{168,40},{176,48},{184,... | collective-permute-start | bytes 786440 | tf_op jit(solution)/shard_map/ppermute | solution.py:14
  119.9 10.4 %collective-permute-start.11 = (f32[4,128,128]{2,1,0:T(8,128)}, f32[4,128,128]{2,1,0:T(8,128)}, u32[]{:S(2)}, u32[]{:S(2)}) collective-permute-start(f32[4,128,128]{2,1,0:T(8,128)} %add.56), channel_id=1, source_target_pairs={{256,0},{264,8},{272,16},{280,24},{288,32},{296,40},{304,48},{312,... | collective-permute-start | bytes 786440 | tf_op jit(solution)/shard_map/ppermute | solution.py:14
  125.4 7.2 %copy-start.2 = (bf16[512,512]{1,0:T(8,128)(2,1)S(1)}, bf16[512,512]{1,0:T(8,128)(2,1)}, u32[]{:S(2)}) copy-start(bf16[512,512]{1,0:T(8,128)(2,1)} %param.5) | copy-start | bytes 1572868
where the time goes:
time: 136 us; the launch traced here: 135 us
  starting transfers between devices  57.9 us (43%)
  waiting for transfers between devices  53.3 us (39%)
  matrix products  10.2 us (7%)
  local copies, waits for them, and re-layouts  6.51 us (5%)
  other arithmetic  6.33 us (5%)
    ppermute x12, waiting for transfers between devices, from_behind(): return lax.ppermute(x, axis, pairs)  53.3 us
    ppermute x12, starting transfers between devices, from_behind(): return lax.ppermute(x, axis, pairs)  50.4 us
    all_to_all x1, starting transfers between devices, local(): lax.all_to_all(out_grad, 'head', split_axis=1, concat_axis=0, tiled=True)  7.55 us
    unnamed x17, local copies, waits for them, and re-layouts  4.1 us
    dot_general x1, matrix products, local(): jnp.einsum('hij,ihe->jhe', attend, grad_rows, preferred_element_type=jnp....  3.32 us
  transfers between devices with their start and end apart: 13, of which 8 were waited for; matrix products, arithmetic and copies ran while one was open for 12% of the time, Pallas kernels for 0%

commit v1 on v0

v1 whole, which is shorter than its diff:
```python
import functools
import math

import jax
import jax.numpy as jnp
from jax import lax
from jax.experimental import pallas as pl
from jax.experimental.pallas import tpu as pltpu
from jax.sharding import PartitionSpec as P

MESH = pl.DeviceIdType.MESH
F32 = jnp.float32
BF16 = jnp.bfloat16

HEAD_DIM = 128
NX, NZ, NCORE, NY = 4, 8, 2, 8
PLANE = NZ * NCORE
ROWS = 16
FAR_FIRST = (4, 3, 5, 2, 6, 1, 7, 0)


def dot(a, b, ca, cb):
    return lax.dot_general(a, b, (((ca,), (cb,)), ((), ())), preferred_element_type=F32)


def kernel(factor, q_hbm, k_hbm, v_hbm, g_hbm, qo_ref, ko_ref, vo_ref,
           q, k, v, g, att, kpart, vpart, qpart,
           kv_stage, kv_land, kv_pre, kv_tot, kv_totland, kv_out, kv_state,
           qg_stage, qg_land, qg_pre, qg_tot, qg_totland, qg_out, qg_state,
           in_sem, a2a_send, a2a_recv, ssem, rsem):
    tokens = q.shape[0]
    half = tokens // 2
    share = g_hbm.shape[0]
    width = q.shape[1]
    c = lax.axis_index("ctx")
    y = lax.axis_index("head")
    x, z, core = c // PLANE, (c // NCORE) % NZ, c % NCORE
    me = c % PLANE

    loads = []
    for i, (src, dst) in enumerate(((k_hbm, k), (v_hbm, v), (q_hbm, q))):
        loads.append(pltpu.make_async_copy(src, dst, in_sem.at[i]))
    loads.append(pltpu.make_async_copy(
        g_hbm.at[:, pl.ds(pl.multiple_of(y * width, width), width)],
        g.at[pl.ds(pl.multiple_of(y * share, share), share), :], in_sem.at[3]))
    for load in loads:
        load.start()

    plane_peers = []
    for d in FAR_FIRST:
        for dc in (1, 0):
            if d or dc:
                pz, pc = (z + d) % NZ, (core + dc) % NCORE
                plane_peers.append((pz, pc))
    barrier = pltpu.get_barrier_semaphore()
    count = 0
    for d in FAR_FIRST[:-1]:
        pl.semaphore_signal(barrier, inc=1, device_id=(c, (y + d) % NY), device_id_type=MESH)
        count += 1
    for pz, pc in plane_peers:
        pl.semaphore_signal(barrier, inc=1, device_id=(x * PLANE + pz * NCORE + pc, y), device_id_type=MESH)
        count += 1
    for d in (2, 1, 3):
        pl.semaphore_signal(barrier, inc=1, device_id=((c + d * PLANE) % (NX * PLANE), y), device_id_type=MESH)
        count += 1
    pl.semaphore_wait(barrier, count)

    for j in range(2):
        for d in FAR_FIRST[:-1]:
            t = (y + d) % NY
            pltpu.make_async_remote_copy(
                src_ref=g_hbm.at[:, pl.ds(pl.multiple_of(t * width + j * 256, 256), 256)],
                dst_ref=g.at[pl.ds(pl.multiple_of(y * share, share), share), pl.ds(j * 256, 256)],
                send_sem=a2a_send.at[j], recv_sem=a2a_recv.at[j],
                device_id=(c, t), device_id_type=MESH).start()

    def wait_bytes(ref, sem):
        pltpu.make_async_copy(ref, ref, sem).wait()

    def cols(h):
        return pl.ds(h * HEAD_DIM, HEAD_DIM)

    def put_stage(stage, e, b, value):
        stage[e, :, b * ROWS:(b + 1) * ROWS, :] = value.astype(BF16).reshape(NZ, ROWS, HEAD_DIM)

    def reduce_start(u, stage, land):
        for pz, pc in plane_peers:
            pltpu.make_async_remote_copy(
                src_ref=stage.at[pc, pz], dst_ref=land.at[me],
                send_sem=ssem.at[u, 0], recv_sem=rsem.at[u, 0],
                device_id=(x * PLANE + pz * NCORE + pc, y), device_id_type=MESH).start()
        land[me] = stage[core, z]

    def reduce_finish(u, land, pre, tot, totland, reverse):
        wait_bytes(land.at[pl.ds(0, PLANE - 1)], rsem.at[u, 0])
        running = jnp.zeros(tot.shape, F32)
        for i in (range(PLANE - 1, -1, -1) if reverse else range(PLANE)):
            pre[i] = running
            running = running + land[i].astype(F32)
        tot[...] = running
        for d in (2, 1, 3):
            pltpu.make_async_remote_copy(
                src_ref=tot, dst_ref=totland.at[x],
                send_sem=ssem.at[u, 1], recv_sem=rsem.at[u, 1],
                device_id=((c + d * PLANE) % (NX * PLANE), y), device_id_type=MESH).start()

    def gather_start(u, pre, tot, totland, out, state, reverse):
        wait_bytes(totland.at[pl.ds(0, NX - 1)], rsem.at[u, 1])
        totland[x] = tot[...]
        far = jnp.zeros(tot.shape, F32)
        for i in range(NX):
            use = (x < i) if reverse else (x > i)
            far = far + jnp.where(use, totland[i], 0.0)
        for i in range(PLANE):
            out[i] = (pre[i] + far).astype(BF16)
        for pz, pc in plane_peers:
            pltpu.make_async_remote_copy(
                src_ref=out.at[pz * NCORE + pc], dst_ref=state.at[core, z],
                send_sem=ssem.at[u, 2], recv_sem=rsem.at[u, 2],
                device_id=(x * PLANE + pz * NCORE + pc, y), device_id_type=MESH).start()
        state[core, z] = out[me]

    def gather_wait(u, land):
        wait_bytes(land.at[pl.ds(0, PLANE - 1)], rsem.at[u, 2])

    def take_state(state, e, b):
        return state[e, :, b * ROWS:(b + 1) * ROWS, :].reshape(HEAD_DIM, HEAD_DIM)

    row = lax.broadcasted_iota(jnp.int32, (half, half), 0)
    col = lax.broadcasted_iota(jnp.int32, (half, half), 1)
    lower, upper = row >= col, col >= row
    lo, hi = pl.ds(0, half), pl.ds(half, half)

    def masked(a, b, mask):
        return jnp.where(mask, dot(a, b, 1, 1), 0.0).astype(BF16)

    loads[0].wait()
    loads[1].wait()
    for h in range(4):
        put_stage(kv_stage, h // 2, h % 2, dot(k[:, cols(h)], v[:, cols(h)], 0, 0))
    reduce_start(0, kv_stage, kv_land)

    loads[2].wait()
    for h in range(4):
        att[h, lo, lo] = masked(k[lo, cols(h)], q[lo, cols(h)], upper)
        att[h, lo, hi] = dot(k[lo, cols(h)], q[hi, cols(h)], 1, 1).astype(BF16)
        att[h, hi, hi] = masked(k[hi, cols(h)], q[hi, cols(h)], upper)
    reduce_finish(0, kv_land, kv_pre, kv_tot, kv_totland, False)

    def query_states(j):
        wait_bytes(g.at[pl.ds(0, tokens - share), pl.ds(j * 256, 256)], a2a_recv.at[j])
        for e in range(2):
            h = 2 * j + e
            put_stage(qg_stage.at[j], e, 0, dot(q[:, cols(h)], g[:, cols(h)], 0, 0))
        reduce_start(1 + j, qg_stage.at[j], qg_land.at[j])

    def within(h):
        up00 = masked(g[lo, cols(h)], v[lo, cols(h)], lower)
        up10 = dot(g[hi, cols(h)], v[lo, cols(h)], 1, 1).astype(BF16)
        up11 = masked(g[hi, cols(h)], v[hi, cols(h)], lower)
        qpart[lo, cols(h)] = dot(up00, k[lo, cols(h)], 1, 0)
        qpart[hi, cols(h)] = dot(up10, k[lo, cols(h)], 1, 0) + dot(up11, k[hi, cols(h)], 1, 0)
        ut00 = masked(v[lo, cols(h)], g[lo, cols(h)], upper)
        ut01 = dot(v[lo, cols(h)], g[hi, cols(h)], 1, 1).astype(BF16)
        ut11 = masked(v[hi, cols(h)], g[hi, cols(h)], upper)
        kpart[lo, cols(h)] = dot(ut00, q[lo, cols(h)], 1, 0) + dot(ut01, q[hi, cols(h)], 1, 0)
        kpart[hi, cols(h)] = dot(ut11, q[hi, cols(h)], 1, 0)
        vpart[lo, cols(h)] = dot(att[h, lo, :], g[:, cols(h)], 1, 0)
        vpart[hi, cols(h)] = dot(att[h, hi, hi], g[hi, cols(h)], 1, 0)

    def finish(h):
        state = take_state(qg_state.at[h // 2], h % 2, 0)
        ko_ref[:, cols(h)] = ((kpart[:, cols(h)] + dot(v[:, cols(h)], state, 1, 1)) * factor).astype(BF16)
        vo_ref[:, cols(h)] = ((vpart[:, cols(h)] + dot(k[:, cols(h)], state, 1, 0)) * factor).astype(BF16)

    loads[3].wait()
    query_states(0)
    gather_start(0, kv_pre, kv_tot, kv_totland, kv_out, kv_state, False)
    query_states(1)
    within(0)
    within(1)
    reduce_finish(1, qg_land.at[0], qg_pre.at[0], qg_tot.at[0], qg_totland.at[0], True)
    within(2)
    within(3)
    gather_wait(0, kv_land)
    for h in range(4):
        state = take_state(kv_state, h // 2, h % 2)
        qo_ref[:, cols(h)] = ((qpart[:, cols(h)] + dot(g[:, cols(h)], state, 1, 1)) * factor).astype(BF16)
    gather_start(1, qg_pre.at[0], qg_tot.at[0], qg_totland.at[0], qg_out.at[0], qg_state.at[0], True)
    reduce_finish(2, qg_land.at[1], qg_pre.at[1], qg_tot.at[1], qg_totland.at[1], True)
    gather_wait(1, qg_land.at[0])
    finish(0)
    finish(1)
    gather_start(2, qg_pre.at[1], qg_tot.at[1], qg_totland.at[1], qg_out.at[1], qg_state.at[1], True)
    gather_wait(2, qg_land.at[1])
    finish(2)
    finish(3)

    for j in range(2):
        wait_bytes(g.at[pl.ds(0, tokens - share), pl.ds(j * 256, 256)], a2a_send.at[j])
    for u, (land, totland) in enumerate((
            (kv_land, kv_totland), (qg_land.at[0], qg_totland.at[0]), (qg_land.at[1], qg_totland.at[1]))):
        wait_bytes(land.at[pl.ds(0, PLANE - 1)], ssem.at[u, 0])
        wait_bytes(totland.at[pl.ds(0, NX - 1)], ssem.at[u, 1])
        wait_bytes(land.at[pl.ds(0, PLANE - 1)], ssem.at[u, 2])


def local(queries, keys, values, out_grad):
    tokens, width = queries.shape
    factor = 1.0 / math.sqrt(HEAD_DIM * tokens * lax.axis_size("ctx"))
    heads = width // HEAD_DIM
    vm = pltpu.VMEM

    def scan_scratch(lead, rows):
        return [
            vm((*lead, NCORE, NZ, rows, HEAD_DIM), BF16),
            vm((*lead, PLANE, rows, HEAD_DIM), BF16),
            vm((*lead, PLANE, rows, HEAD_DIM), F32),
            vm((*lead, rows, HEAD_DIM), F32),
            vm((*lead, NX, rows, HEAD_DIM), F32),
            vm((*lead, PLANE, rows, HEAD_DIM), BF16),
            vm((*lead, NCORE, NZ, rows, HEAD_DIM), BF16),
        ]

    dma = pltpu.SemaphoreType.DMA
    out = jax.ShapeDtypeStruct((tokens, width), BF16)
    return pl.pallas_call(
        functools.partial(kernel, factor),
        out_shape=(out, out, out),
        in_specs=[pl.BlockSpec(memory_space=pl.ANY)] * 4,
        out_specs=[pl.BlockSpec(memory_space=pltpu.VMEM)] * 3,
        scratch_shapes=[
            *[vm((tokens, width), BF16)] * 4,
            vm((heads, tokens, tokens), BF16),
            *[vm((tokens, width), F32)] * 3,
            *scan_scratch((), 2 * ROWS),
            *scan_scratch((2,), ROWS),
            dma((4,)), dma((2,)), dma((2,)), dma((3, 3)), dma((3, 3)),
        ],
        compiler_params=pltpu.CompilerParams(
            collective_id=0, has_side_effects=True, vmem_limit_bytes=56 * 2**20),
    )(queries, keys, values, out_grad)


def solution(mesh):
    return jax.shard_map(
        local,
        mesh=mesh,
        in_specs=(P("ctx", "head"), P("ctx", "head"), P("ctx", "head"), P(("ctx", "head"), None)),
        out_specs=(P("ctx", "head"), P("ctx", "head"), P("ctx", "head")),
        check_vma=False,
    )
```

time: 136 us -> 49.9 us (0.37)
  the two profiles are of different devices: /device:TPU:72 before, /device:TPU:1 now
where the time goes in v1:
time: 49.9 us; the launch traced here: 49.7 us
  Pallas kernels  45.1 us (90%)
  local copies, waits for them, and re-layouts  3.95 us (8%)
  between operations  0.65 us (1%)
    pallas_call x1, Pallas kernels, local(): pl.pallas_call(functools.partial(kernel, factor), out_shape=(out, out, ou...  45.1 us
    unnamed x7, local copies, waits for them, and re-layouts  3.95 us

profile of v1, /device:TPU:1, one launch (start us, length us, event | category | flops | bytes accessed | tf_op | source)
XLA Modules:
  0.0 49.7 jit_solution(11687642822380774675)
XLA Ops:
  0.6 45.1 %shard_map.67 = (bf16[512,512]{1,0:T(8,128)(2,1)}, bf16[512,512]{1,0:T(8,128)(2,1)}, bf16[512,512]{1,0:T(8,128)(2,1)}) custom-call(bf16[512,512]{1,0:T(8,128)(2,1)} %q_hbm.1, bf16[512,512]{1,0:T(8,128)(2,1)} %k_hbm.1, bf16[512,512]{1,0:T(8,128)(2,1)} %v_hbm.1, bf16[64,4096]{1,0:T(8,128)(2,1)} %g_hbm.1), custom_call_target="tpu_custom_call" | custom-call | tf_op jit(solution)/shard_map/pallas_call | solution.py:227
  45.7 0.0 copy-start.1
  45.7 1.9 %copy.10 = bf16[512,512]{1,0:T(8,128)(2,1)} copy(bf16[512,512]{1,0:T(8,128)(2,1)} %get-tuple-element.6) | data formatting | bytes 1048576
  47.7 0.0 copy-done.1
  47.7 0.0 copy-start
  47.7 0.8 %copy.11 = bf16[512,512]{1,0:T(8,128)(2,1)} copy(bf16[512,512]{1,0:T(8,128)(2,1)S(1)} %copy-done.1) | data formatting | bytes 1048576
  48.5 0.4 copy-done
  48.9 0.8 %copy.12 = bf16[512,512]{1,0:T(8,128)(2,1)} copy(bf16[512,512]{1,0:T(8,128)(2,1)S(1)} %copy-done) | data formatting | bytes 1048576
Async XLA Ops:
  45.7 1.9 %copy-start.1 = (bf16[512,512]{1,0:T(8,128)(2,1)S(1)}, bf16[512,512]{1,0:T(8,128)(2,1)}, u32[]{:S(2)}) copy-start(bf16[512,512]{1,0:T(8,128)(2,1)} %get-tuple-element.7) | copy-start | bytes 1572868
  47.7 1.2 %copy-start = (bf16[512,512]{1,0:T(8,128)(2,1)S(1)}, bf16[512,512]{1,0:T(8,128)(2,1)}, u32[]{:S(2)}) copy-start(bf16[512,512]{1,0:T(8,128)(2,1)} %get-tuple-element.8) | copy-start | bytes 1572868

commit v2 on v1

v2 whole, which is shorter than its diff:
```python
import functools
import math

import jax
import jax.numpy as jnp
from jax import lax
from jax.experimental import pallas as pl
from jax.experimental.pallas import tpu as pltpu
from jax.sharding import PartitionSpec as P

MESH = pl.DeviceIdType.MESH
F32 = jnp.float32
BF16 = jnp.bfloat16

HEAD_DIM = 128
NX, NZ, NCORE, NY = 4, 8, 2, 8
PLANE = NZ * NCORE
ROWS = 16
FAR_FIRST = (4, 3, 5, 2, 6, 1, 7, 0)
OWNERS = (6, 7, 0, 1)
CHUNKS = ((0, 256), (256, 128), (384, 128))


def dot(a, b, ca, cb):
    return lax.dot_general(a, b, (((ca,), (cb,)), ((), ())), preferred_element_type=F32)


def kernel(factor, q_hbm, k_hbm, v_hbm, g_hbm, qo_ref, ko_ref, vo_ref,
           q, k, v, g, att, kpart, vpart, qpart,
           kv_stage, kv_land, kv_pre, kv_tot, kv_totland, kv_out, kv_state,
           qg_stage, qg_land, qg_pre, qg_tot, qg_totland, qg_out, qg_state,
           last_stage, last_land, last_pre, last_tot, last_totland, last_out, last_state,
           in_sem, a2a_send, a2a_recv, ssem, rsem):
    tokens = q.shape[0]
    half = tokens // 2
    share = g_hbm.shape[0]
    width = q.shape[1]
    c = lax.axis_index("ctx")
    y = lax.axis_index("head")
    x, z, core = c // PLANE, (c // NCORE) % NZ, c % NCORE
    me = c % PLANE

    mine = jnp.int32(-1)
    for p in range(NZ):
        mine = jnp.where(me == OWNERS[p // 2] * NCORE + p % 2, p, mine)
    owner = mine >= 0
    piece = jnp.maximum(mine, 0)

    loads = []
    for i, (src, dst) in enumerate(((k_hbm, k), (v_hbm, v), (q_hbm, q))):
        loads.append(pltpu.make_async_copy(src, dst, in_sem.at[i]))
    loads.append(pltpu.make_async_copy(
        g_hbm.at[:, pl.ds(pl.multiple_of(y * width, width), width)],
        g.at[pl.ds(pl.multiple_of(y * share, share), share), :], in_sem.at[3]))
    for load in loads:
        load.start()

    plane_peers = []
    for d in FAR_FIRST:
        for dc in (1, 0):
            if d or dc:
                pz, pc = (z + d) % NZ, (core + dc) % NCORE
                plane_peers.append((pz, pc))
    barrier = pltpu.get_barrier_semaphore()
    count = 0
    for d in FAR_FIRST[:-1]:
        pl.semaphore_signal(barrier, inc=1, device_id=(c, (y + d) % NY), device_id_type=MESH)
        count += 1
    for pz, pc in plane_peers:
        pl.semaphore_signal(barrier, inc=1, device_id=(x * PLANE + pz * NCORE + pc, y), device_id_type=MESH)
        count += 1
    for d in (2, 1, 3):
        pl.semaphore_signal(barrier, inc=1, device_id=((c + d * PLANE) % (NX * PLANE), y), device_id_type=MESH)
        count += 1

    def wait_bytes(ref, sem):
        pltpu.make_async_copy(ref, ref, sem).wait()

    def cols(h):
        return pl.ds(h * HEAD_DIM, HEAD_DIM)

    def put_stage(stage, e, b, value):
        stage[e, :, b * ROWS:(b + 1) * ROWS, :] = value.astype(BF16).reshape(NZ, ROWS, HEAD_DIM)

    row = lax.broadcasted_iota(jnp.int32, (half, half), 0)
    col = lax.broadcasted_iota(jnp.int32, (half, half), 1)
    lower, upper = row >= col, col >= row
    lo, hi = pl.ds(0, half), pl.ds(half, half)

    def masked(a, b, mask):
        return jnp.where(mask, dot(a, b, 1, 1), 0.0).astype(BF16)

    loads[0].wait()
    loads[1].wait()
    for h in range(4):
        put_stage(kv_stage, h // 2, h % 2, dot(k[:, cols(h)], v[:, cols(h)], 0, 0))
    loads[2].wait()
    loads[3].wait()
    pl.semaphore_wait(barrier, count)

    for j, (at, wide) in enumerate(CHUNKS):
        for d in FAR_FIRST[:-1]:
            t = (y + d) % NY
            pltpu.make_async_remote_copy(
                src_ref=g_hbm.at[:, pl.ds(pl.multiple_of(t * width + at, HEAD_DIM), wide)],
                dst_ref=g.at[pl.ds(pl.multiple_of(y * share, share), share), pl.ds(at, wide)],
                send_sem=a2a_send.at[j], recv_sem=a2a_recv.at[j],
                device_id=(c, t), device_id_type=MESH).start()

    def a2a_wait(j, sem):
        at, wide = CHUNKS[j]
        wait_bytes(g.at[pl.ds(0, tokens - share), pl.ds(at, wide)], sem.at[j])

    def remote(src, dst, u, step, pz, pc):
        return pltpu.make_async_remote_copy(
            src_ref=src, dst_ref=dst, send_sem=ssem.at[u, step], recv_sem=rsem.at[u, step],
            device_id=(x * PLANE + pz * NCORE + pc, y), device_id_type=MESH)

    def reduce_start(u, stage, land):
        for pz, pc in plane_peers:
            remote(stage.at[pc, pz], land.at[me], u, 0, pz, pc).start()
        land[me] = stage[core, z]

    def reduce_sum(u, land, pre, tot, totland, reverse):
        running = jnp.zeros(tot.shape, F32)
        for i in (range(PLANE - 1, -1, -1) if reverse else range(PLANE)):
            pre[i] = running
            running = running + land[i].astype(F32)
        tot[...] = running
        for d in (2, 1, 3):
            pltpu.make_async_remote_copy(
                src_ref=tot, dst_ref=totland.at[x],
                send_sem=ssem.at[u, 1], recv_sem=rsem.at[u, 1],
                device_id=((c + d * PLANE) % (NX * PLANE), y), device_id_type=MESH).start()

    def reduce_finish(u, land, pre, tot, totland, reverse):
        wait_bytes(land.at[pl.ds(0, PLANE - 1)], rsem.at[u, 0])
        reduce_sum(u, land, pre, tot, totland, reverse)

    def gather_send(u, pre, tot, totland, out, dst, reverse):
        wait_bytes(totland.at[pl.ds(0, NX - 1)], rsem.at[u, 1])
        totland[x] = tot[...]
        far = jnp.zeros(tot.shape, F32)
        for i in range(NX):
            use = (x < i) if reverse else (x > i)
            far = far + jnp.where(use, totland[i], 0.0)
        for pz, pc in plane_peers:
            t = pz * NCORE + pc
            out[t] = (pre[t] + far).astype(BF16)
            remote(out.at[t], dst, u, 2, pz, pc).start()
        return (pre[me] + far).astype(BF16)

    def gather_start(u, pre, tot, totland, out, state, reverse):
        state[core, z] = gather_send(u, pre, tot, totland, out, state.at[core, z], reverse)

    def gather_wait(u, land):
        wait_bytes(land.at[pl.ds(0, PLANE - 1)], rsem.at[u, 2])

    def last_reduce_start(u, stage, land):
        for p in range(NZ):
            pz, pc = OWNERS[p // 2], p % 2

            @pl.when(mine != p)
            def _():
                remote(stage.at[p], land.at[me], u, 0, pz, pc).start()

        @pl.when(owner)
        def _():
            land[me] = stage[piece]

    def last_reduce_finish(u, land, pre, tot, totland):
        @pl.when(owner)
        def _():
            reduce_finish(u, land, pre, tot, totland, True)

    def last_gather_start(u, pre, tot, totland, out, state):
        @pl.when(owner)
        def _():
            state[piece] = gather_send(u, pre, tot, totland, out, state.at[piece], True)

    def last_wait(state, sem):
        @pl.when(owner)
        def _():
            wait_bytes(state.at[pl.ds(0, NZ - 1)], sem)

        @pl.when(jnp.logical_not(owner))
        def _():
            wait_bytes(state, sem)

    reduce_start(0, kv_stage, kv_land)

    for h in range(4):
        att[h, lo, lo] = masked(k[lo, cols(h)], q[lo, cols(h)], upper)
        att[h, lo, hi] = dot(k[lo, cols(h)], q[hi, cols(h)], 1, 1).astype(BF16)
        att[h, hi, hi] = masked(k[hi, cols(h)], q[hi, cols(h)], upper)
    reduce_finish(0, kv_land, kv_pre, kv_tot, kv_totland, False)

    def query_state(h):
        return dot(q[:, cols(h)], g[:, cols(h)], 0, 0)

    def within(h):
        up00 = masked(g[lo, cols(h)], v[lo, cols(h)], lower)
        up10 = dot(g[hi, cols(h)], v[lo, cols(h)], 1, 1).astype(BF16)
        up11 = masked(g[hi, cols(h)], v[hi, cols(h)], lower)
        qpart[lo, cols(h)] = dot(up00, k[lo, cols(h)], 1, 0)
        qpart[hi, cols(h)] = dot(up10, k[lo, cols(h)], 1, 0) + dot(up11, k[hi, cols(h)], 1, 0)
        ut00 = masked(v[lo, cols(h)], g[lo, cols(h)], upper)
        ut01 = dot(v[lo, cols(h)], g[hi, cols(h)], 1, 1).astype(BF16)
        ut11 = masked(v[hi, cols(h)], g[hi, cols(h)], upper)
        kpart[lo, cols(h)] = dot(ut00, q[lo, cols(h)], 1, 0) + dot(ut01, q[hi, cols(h)], 1, 0)
        kpart[hi, cols(h)] = dot(ut11, q[hi, cols(h)], 1, 0)
        vpart[lo, cols(h)] = dot(att[h, lo, :], g[:, cols(h)], 1, 0)
        vpart[hi, cols(h)] = dot(att[h, hi, hi], g[hi, cols(h)], 1, 0)

    def finish(h, state):
        ko_ref[:, cols(h)] = ((kpart[:, cols(h)] + dot(v[:, cols(h)], state, 1, 1)) * factor).astype(BF16)
        vo_ref[:, cols(h)] = ((vpart[:, cols(h)] + dot(k[:, cols(h)], state, 1, 0)) * factor).astype(BF16)

    def last(ref):
        return [r.at[ref] for r in (last_stage, last_land, last_pre, last_tot, last_totland, last_out, last_state)]

    a2a_wait(0, a2a_recv)
    for h in range(2):
        put_stage(qg_stage, h, 0, query_state(h))
    reduce_start(1, qg_stage, qg_land)
    gather_start(0, kv_pre, kv_tot, kv_totland, kv_out, kv_state, False)

    def last_states(i):
        a2a_wait(1 + i, a2a_recv)
        stage, land = last(i)[:2]
        stage[...] = query_state(2 + i).astype(BF16).reshape(NZ, ROWS, HEAD_DIM)
        last_reduce_start(2 + i, stage, land)

    last_states(0)
    within(0)
    last_states(1)
    reduce_finish(1, qg_land, qg_pre, qg_tot, qg_totland, True)
    within(1)
    last_reduce_finish(2, *last(0)[1:5])
    within(2)
    gather_start(1, qg_pre, qg_tot, qg_totland, qg_out, qg_state, True)
    within(3)
    last_reduce_finish(3, *last(1)[1:5])
    last_gather_start(2, *last(0)[2:])
    gather_wait(0, kv_land)
    for h in range(4):
        b = h % 2
        state = kv_state[h // 2, :, b * ROWS:(b + 1) * ROWS, :].reshape(HEAD_DIM, HEAD_DIM)
        qo_ref[:, cols(h)] = ((qpart[:, cols(h)] + dot(g[:, cols(h)], state, 1, 1)) * factor).astype(BF16)
    last_gather_start(3, *last(1)[2:])
    gather_wait(1, qg_land)
    for h in range(2):
        finish(h, qg_state[h].reshape(HEAD_DIM, HEAD_DIM))
    for i in range(2):
        last_wait(last_state.at[i], rsem.at[2 + i, 2])
        finish(2 + i, last_state[i].reshape(HEAD_DIM, HEAD_DIM))

    for j in range(3):
        a2a_wait(j, a2a_send)
    for u, (land, totland) in enumerate(((kv_land, kv_totland), (qg_land, qg_totland))):
        wait_bytes(land.at[pl.ds(0, PLANE - 1)], ssem.at[u, 0])
        wait_bytes(totland.at[pl.ds(0, NX - 1)], ssem.at[u, 1])
        wait_bytes(land.at[pl.ds(0, PLANE - 1)], ssem.at[u, 2])
    for i in range(2):
        last_wait(last_state.at[i], ssem.at[2 + i, 0])

    @pl.when(owner)
    def _():
        for i in range(2):
            wait_bytes(last_totland.at[i, pl.ds(0, NX - 1)], ssem.at[2 + i, 1])
            wait_bytes(last_land.at[i, pl.ds(0, PLANE - 1)], ssem.at[2 + i, 2])


def store(qo_ref, ko_ref, vo_ref, q_hbm, k_hbm, v_hbm, sem):
    copies = [pltpu.make_async_copy(src, dst, sem.at[i]) for i, (src, dst) in enumerate(
        ((qo_ref, q_hbm), (ko_ref, k_hbm), (vo_ref, v_hbm)))]
    for copy in copies:
        copy.start()
    for copy in copies:
        copy.wait()


def local(queries, keys, values, out_grad):
    tokens, width = queries.shape
    factor = 1.0 / math.sqrt(HEAD_DIM * tokens * lax.axis_size("ctx"))
    heads = width // HEAD_DIM
    vm = pltpu.VMEM

    def scan_scratch(lead, rows):
        return [
            vm((*lead, NCORE, NZ, rows, HEAD_DIM), BF16),
            vm((*lead, PLANE, rows, HEAD_DIM), BF16),
            vm((*lead, PLANE, rows, HEAD_DIM), F32),
            vm((*lead, rows, HEAD_DIM), F32),
            vm((*lead, NX, rows, HEAD_DIM), F32),
            vm((*lead, PLANE, rows, HEAD_DIM), BF16),
            vm((*lead, NCORE, NZ, rows, HEAD_DIM), BF16),
        ]

    dma = pltpu.SemaphoreType.DMA
    last = scan_scratch((2,), ROWS)
    for at in (0, -1):
        last[at] = vm((2, NZ, ROWS, HEAD_DIM), BF16)
    grads = pl.pallas_call(
        functools.partial(kernel, factor),
        out_shape=(vm((tokens, width), BF16),) * 3,
        in_specs=[pl.BlockSpec(memory_space=pltpu.HBM)] * 4,
        out_specs=[pl.BlockSpec(memory_space=pltpu.VMEM)] * 3,
        scratch_shapes=[
            *[vm((tokens, width), BF16)] * 4,
            vm((heads, tokens, tokens), BF16),
            *[vm((tokens, width), F32)] * 3,
            *scan_scratch((), 2 * ROWS),
            *scan_scratch((), ROWS),
            *last,
            dma((4,)), dma((3,)), dma((3,)), dma((4, 3)), dma((4, 3)),
        ],
        compiler_params=pltpu.CompilerParams(
            collective_id=0, has_side_effects=True, vmem_limit_bytes=20 * 2**20),
    )(*(pltpu.with_memory_space_constraint(a, pltpu.HBM) for a in (queries, keys, values, out_grad)))
    return pl.pallas_call(
        store,
        out_shape=(pltpu.HBM((tokens, width), BF16),) * 3,
        in_specs=[pl.BlockSpec(memory_space=pltpu.VMEM)] * 3,
        out_specs=[pl.BlockSpec(memory_space=pltpu.HBM)] * 3,
        scratch_shapes=[dma((3,))],
    )(*(pltpu.with_memory_space_constraint(a, pltpu.VMEM) for a in grads))


def solution(mesh):
    return jax.shard_map(
        local,
        mesh=mesh,
        in_specs=(P("ctx", "head"), P("ctx", "head"), P("ctx", "head"), P(("ctx", "head"), None)),
        out_specs=(P("ctx", "head"), P("ctx", "head"), P("ctx", "head")),
        check_vma=False,
    )
```

time: 49.9 us -> 45.1 us (0.904)
  local copies, waits for them, and re-layouts: 3.95 us -> 0 us
  Pallas kernels: 45.1 us -> 44.3 us
    unnamed x7 -> x0, local copies, waits for them, and re-layouts: 3.95 us -> none
    pallas_call x1 -> x2, Pallas kernels: 45.1 us -> 44.3 us  [the longest x1 43.2 us: local(): pl.pallas_call(functools.partial(kernel, factor), out_shape=(vm((tokens,...]
where the time goes in v2:
time: 45.1 us; the launch traced here: 45 us
  Pallas kernels  44.3 us (98%)
  between operations  0.64 us (1%)
    pallas_call x1, Pallas kernels, local(): pl.pallas_call(functools.partial(kernel, factor), out_shape=(vm((tokens,...  43.2 us
    pallas_call x1, Pallas kernels, local(): pl.pallas_call(store, out_shape=(pltpu.HBM((tokens, width), BF16),) * 3,...  1.17 us

profile of v2, /device:TPU:1, one launch (start us, length us, event | category | flops | bytes accessed | tf_op | source)
XLA Modules:
  0.0 45.0 jit_solution(238407625131898896)
XLA Ops:
  0.6 43.2 %shard_map.67 = (bf16[512,512]{1,0:T(8,128)(2,1)S(1)}, bf16[512,512]{1,0:T(8,128)(2,1)S(1)}, bf16[512,512]{1,0:T(8,128)(2,1)S(1)}) custom-call(bf16[512,512]{1,0:T(8,128)(2,1)} %q_hbm.1, bf16[512,512]{1,0:T(8,128)(2,1)} %k_hbm.1, bf16[512,512]{1,0:T(8,128)(2,1)} %v_hbm.1, bf16[64,4096]{1,0:T(8,128)(2,1)} %g_hbm.1), custom_call_target="tpu_custom_call" | custom-call | tf_op jit(solution)/shard_map/pallas_call | solution.py:304
  43.8 1.2 %shard_map.68 = (bf16[512,512]{1,0:T(8,128)(2,1)}, bf16[512,512]{1,0:T(8,128)(2,1)}, bf16[512,512]{1,0:T(8,128)(2,1)}) custom-call(bf16[512,512]{1,0:T(8,128)(2,1)S(1)} %get-tuple-element.6.qo_ref, bf16[512,512]{1,0:T(8,128)(2,1)S(1)} %get-tuple-element.7.ko_ref, bf16[512,512]{1,0:T(8,128)(2,1)S(1)} %get-tuple-element.8.vo_ref), custom_call_target="tpu_custom_call" | custom-call | tf_op jit(solution)/shard_map/pallas_call | solution.py:321

commit v3 on v2

--- a/solution.py
+++ b/solution.py
@@ -17,7 +17,9 @@
 PLANE = NZ * NCORE
 ROWS = 16
 FAR_FIRST = (4, 3, 5, 2, 6, 1, 7, 0)
-OWNERS = (6, 7, 0, 1)
+OWNERS = tuple((z, core) for z in range(4) for core in range(2))
+PIECES = len(OWNERS)
+LAST_ROWS = HEAD_DIM // PIECES
 CHUNKS = ((0, 256), (256, 128), (384, 128))
 
 
@@ -41,8 +43,8 @@
     me = c % PLANE
 
     mine = jnp.int32(-1)
-    for p in range(NZ):
-        mine = jnp.where(me == OWNERS[p // 2] * NCORE + p % 2, p, mine)
+    for p, (pz, pc) in enumerate(OWNERS):
+        mine = jnp.where(me == pz * NCORE + pc, p, mine)
     owner = mine >= 0
     piece = jnp.maximum(mine, 0)
 
@@ -157,9 +159,7 @@
         wait_bytes(land.at[pl.ds(0, PLANE - 1)], rsem.at[u, 2])
 
     def last_reduce_start(u, stage, land):
-        for p in range(NZ):
-            pz, pc = OWNERS[p // 2], p % 2
-
+        for p, (pz, pc) in enumerate(OWNERS):
             @pl.when(mine != p)
             def _():
                 remote(stage.at[p], land.at[me], u, 0, pz, pc).start()
@@ -181,7 +181,7 @@
     def last_wait(state, sem):
         @pl.when(owner)
         def _():
-            wait_bytes(state.at[pl.ds(0, NZ - 1)], sem)
+            wait_bytes(state.at[pl.ds(0, PIECES - 1)], sem)
 
         @pl.when(jnp.logical_not(owner))
         def _():
@@ -228,7 +228,7 @@
     def last_states(i):
         a2a_wait(1 + i, a2a_recv)
         stage, land = last(i)[:2]
-        stage[...] = query_state(2 + i).astype(BF16).reshape(NZ, ROWS, HEAD_DIM)
+        stage[...] = query_state(2 + i).astype(BF16).reshape(PIECES, LAST_ROWS, HEAD_DIM)
         last_reduce_start(2 + i, stage, land)
 
     last_states(0)
@@ -237,17 +237,17 @@
     reduce_finish(1, qg_land, qg_pre, qg_tot, qg_totland, True)
     within(1)
     last_reduce_finish(2, *last(0)[1:5])
+    gather_start(1, qg_pre, qg_tot, qg_totland, qg_out, qg_state, True)
+    last_reduce_finish(3, *last(1)[1:5])
     within(2)
-    gather_start(1, qg_pre, qg_tot, qg_totland, qg_out, qg_state, True)
+    last_gather_start(2, *last(0)[2:])
+    last_gather_start(3, *last(1)[2:])
     within(3)
-    last_reduce_finish(3, *last(1)[1:5])
-    last_gather_start(2, *last(0)[2:])
     gather_wait(0, kv_land)
     for h in range(4):
         b = h % 2
         state = kv_state[h // 2, :, b * ROWS:(b + 1) * ROWS, :].reshape(HEAD_DIM, HEAD_DIM)
         qo_ref[:, cols(h)] = ((qpart[:, cols(h)] + dot(g[:, cols(h)], state, 1, 1)) * factor).astype(BF16)
-    last_gather_start(3, *last(1)[2:])
     gather_wait(1, qg_land)
     for h in range(2):
         finish(h, qg_state[h].reshape(HEAD_DIM, HEAD_DIM))
@@ -298,9 +298,9 @@
         ]
 
     dma = pltpu.SemaphoreType.DMA
-    last = scan_scratch((2,), ROWS)
+    last = scan_scratch((2,), LAST_ROWS)
     for at in (0, -1):
-        last[at] = vm((2, NZ, ROWS, HEAD_DIM), BF16)
+        last[at] = vm((2, PIECES, LAST_ROWS, HEAD_DIM), BF16)
     grads = pl.pallas_call(
         functools.partial(kernel, factor),
         out_shape=(vm((tokens, width), BF16),) * 3,

time: 45.1 us -> 43.3 us (0.960)
  Pallas kernels: 44.3 us -> 42.5 us
    pallas_call x1, Pallas kernels: 43.2 us -> 41.3 us  [local(): pl.pallas_call(functools.partial(kernel, factor), out_shape=(vm((tokens,...]
where the time goes in v3:
time: 43.3 us; the launch traced here: 43.2 us
  Pallas kernels  42.5 us (98%)
  between operations  0.64 us (1%)
    pallas_call x1, Pallas kernels, local(): pl.pallas_call(functools.partial(kernel, factor), out_shape=(vm((tokens,...  41.3 us
    pallas_call x1, Pallas kernels, local(): pl.pallas_call(store, out_shape=(pltpu.HBM((tokens, width), BF16),) * 3,...  1.17 us

profile of v3, /device:TPU:1, one launch (start us, length us, event | category | flops | bytes accessed | tf_op | source)
XLA Modules:
  0.0 43.2 jit_solution(16997936926249519879)
XLA Ops:
  0.6 41.3 %shard_map.67 = (bf16[512,512]{1,0:T(8,128)(2,1)S(1)}, bf16[512,512]{1,0:T(8,128)(2,1)S(1)}, bf16[512,512]{1,0:T(8,128)(2,1)S(1)}) custom-call(bf16[512,512]{1,0:T(8,128)(2,1)} %q_hbm.1, bf16[512,512]{1,0:T(8,128)(2,1)} %k_hbm.1, bf16[512,512]{1,0:T(8,128)(2,1)} %v_hbm.1, bf16[64,4096]{1,0:T(8,128)(2,1)} %g_hbm.1), custom_call_target="tpu_custom_call" | custom-call | tf_op jit(solution)/shard_map/pallas_call | solution.py:304
  42.0 1.2 %shard_map.68 = (bf16[512,512]{1,0:T(8,128)(2,1)}, bf16[512,512]{1,0:T(8,128)(2,1)}, bf16[512,512]{1,0:T(8,128)(2,1)}) custom-call(bf16[512,512]{1,0:T(8,128)(2,1)S(1)} %get-tuple-element.6.qo_ref, bf16[512,512]{1,0:T(8,128)(2,1)S(1)} %get-tuple-element.7.ko_ref, bf16[512,512]{1,0:T(8,128)(2,1)S(1)} %get-tuple-element.8.vo_ref), custom_call_target="tpu_custom_call" | custom-call | tf_op jit(solution)/shard_map/pallas_call | solution.py:321

commit v4 on v3

--- a/solution.py
+++ b/solution.py
@@ -28,7 +28,7 @@
 
 
 def kernel(factor, q_hbm, k_hbm, v_hbm, g_hbm, qo_ref, ko_ref, vo_ref,
-           q, k, v, g, att, kpart, vpart, qpart,
+           q, k, v, g, q_flip, att, kpart, vpart, qpart,
            kv_stage, kv_land, kv_pre, kv_tot, kv_totland, kv_out, kv_state,
            qg_stage, qg_land, qg_pre, qg_tot, qg_totland, qg_out, qg_state,
            last_stage, last_land, last_pre, last_tot, last_totland, last_out, last_state,
@@ -193,6 +193,8 @@
         att[h, lo, lo] = masked(k[lo, cols(h)], q[lo, cols(h)], upper)
         att[h, lo, hi] = dot(k[lo, cols(h)], q[hi, cols(h)], 1, 1).astype(BF16)
         att[h, hi, hi] = masked(k[hi, cols(h)], q[hi, cols(h)], upper)
+    for i in range(2):
+        q_flip[i] = q[:, cols(2 + i)].T
     reduce_finish(0, kv_land, kv_pre, kv_tot, kv_totland, False)
 
     def query_state(h):
@@ -228,17 +230,17 @@
     def last_states(i):
         a2a_wait(1 + i, a2a_recv)
         stage, land = last(i)[:2]
-        stage[...] = query_state(2 + i).astype(BF16).reshape(PIECES, LAST_ROWS, HEAD_DIM)
+        stage[...] = dot(q_flip[i], g[:, cols(2 + i)], 1, 0).astype(BF16).reshape(PIECES, LAST_ROWS, HEAD_DIM)
         last_reduce_start(2 + i, stage, land)
 
+    within(0)
     last_states(0)
-    within(0)
     last_states(1)
     reduce_finish(1, qg_land, qg_pre, qg_tot, qg_totland, True)
     within(1)
     last_reduce_finish(2, *last(0)[1:5])
+    last_reduce_finish(3, *last(1)[1:5])
     gather_start(1, qg_pre, qg_tot, qg_totland, qg_out, qg_state, True)
-    last_reduce_finish(3, *last(1)[1:5])
     within(2)
     last_gather_start(2, *last(0)[2:])
     last_gather_start(3, *last(1)[2:])
@@ -251,9 +253,8 @@
     gather_wait(1, qg_land)
     for h in range(2):
         finish(h, qg_state[h].reshape(HEAD_DIM, HEAD_DIM))
-    for i in range(2):
-        last_wait(last_state.at[i], rsem.at[2 + i, 2])
-        finish(2 + i, last_state[i].reshape(HEAD_DIM, HEAD_DIM))
+    last_wait(last_state.at[0], rsem.at[2, 2])
+    finish(2, last_state[0].reshape(HEAD_DIM, HEAD_DIM))
 
     for j in range(3):
         a2a_wait(j, a2a_send)
@@ -268,7 +269,14 @@
     def _():
         for i in range(2):
             wait_bytes(last_totland.at[i, pl.ds(0, NX - 1)], ssem.at[2 + i, 1])
-            wait_bytes(last_land.at[i, pl.ds(0, PLANE - 1)], ssem.at[2 + i, 2])
+        wait_bytes(last_land.at[0, pl.ds(0, PLANE - 1)], ssem.at[2, 2])
+
+    last_wait(last_state.at[1], rsem.at[3, 2])
+    finish(3, last_state[1].reshape(HEAD_DIM, HEAD_DIM))
+
+    @pl.when(owner)
+    def _():
+        wait_bytes(last_land.at[1, pl.ds(0, PLANE - 1)], ssem.at[3, 2])
 
 
 def store(qo_ref, ko_ref, vo_ref, q_hbm, k_hbm, v_hbm, sem):
@@ -308,6 +316,7 @@
         out_specs=[pl.BlockSpec(memory_space=pltpu.VMEM)] * 3,
         scratch_shapes=[
             *[vm((tokens, width), BF16)] * 4,
+            vm((2, HEAD_DIM, tokens), BF16),
             vm((heads, tokens, tokens), BF16),
             *[vm((tokens, width), F32)] * 3,
             *scan_scratch((), 2 * ROWS),

time: 43.3 us -> 43 us (level)
  no operation moved by 1% of the time
where the time goes in v4:
time: 43 us; the launch traced here: 42.9 us
  Pallas kernels  42.3 us (98%)
  between operations  0.64 us (1%)
    pallas_call x1, Pallas kernels, local(): pl.pallas_call(functools.partial(kernel, factor), out_shape=(vm((tokens,...  41.1 us
    pallas_call x1, Pallas kernels, local(): pl.pallas_call(store, out_shape=(pltpu.HBM((tokens, width), BF16),) * 3,...  1.17 us

profile of v4, /device:TPU:1, one launch (start us, length us, event | category | flops | bytes accessed | tf_op | source)
XLA Modules:
  0.0 42.9 jit_solution(579630820225681432)
XLA Ops:
  0.6 41.1 %shard_map.67 = (bf16[512,512]{1,0:T(8,128)(2,1)S(1)}, bf16[512,512]{1,0:T(8,128)(2,1)S(1)}, bf16[512,512]{1,0:T(8,128)(2,1)S(1)}) custom-call(bf16[512,512]{1,0:T(8,128)(2,1)} %q_hbm.1, bf16[512,512]{1,0:T(8,128)(2,1)} %k_hbm.1, bf16[512,512]{1,0:T(8,128)(2,1)} %v_hbm.1, bf16[64,4096]{1,0:T(8,128)(2,1)} %g_hbm.1), custom_call_target="tpu_custom_call" | custom-call | tf_op jit(solution)/shard_map/pallas_call | solution.py:312
  41.7 1.2 %shard_map.68 = (bf16[512,512]{1,0:T(8,128)(2,1)}, bf16[512,512]{1,0:T(8,128)(2,1)}, bf16[512,512]{1,0:T(8,128)(2,1)}) custom-call(bf16[512,512]{1,0:T(8,128)(2,1)S(1)} %get-tuple-element.6.qo_ref, bf16[512,512]{1,0:T(8,128)(2,1)S(1)} %get-tuple-element.7.ko_ref, bf16[512,512]{1,0:T(8,128)(2,1)S(1)} %get-tuple-element.8.vo_ref), custom_call_target="tpu_custom_call" | custom-call | tf_op jit(solution)/shard_map/pallas_call | solution.py:330

commit v5 on v4

--- a/solution.py
+++ b/solution.py
@@ -124,16 +124,19 @@
         land[me] = stage[core, z]
 
     def reduce_sum(u, land, pre, tot, totland, reverse):
-        running = jnp.zeros(tot.shape, F32)
-        for i in (range(PLANE - 1, -1, -1) if reverse else range(PLANE)):
-            pre[i] = running
-            running = running + land[i].astype(F32)
-        tot[...] = running
+        parts = [land[i].astype(F32) for i in range(PLANE)]
+        while len(parts) > 1:
+            parts = [m + n for m, n in zip(parts[::2], parts[1::2])]
+        tot[...] = parts[0]
         for d in (2, 1, 3):
             pltpu.make_async_remote_copy(
                 src_ref=tot, dst_ref=totland.at[x],
                 send_sem=ssem.at[u, 1], recv_sem=rsem.at[u, 1],
                 device_id=((c + d * PLANE) % (NX * PLANE), y), device_id_type=MESH).start()
+        running = jnp.zeros(tot.shape, F32)
+        for i in (range(PLANE - 1, -1, -1) if reverse else range(PLANE)):
+            pre[i] = running
+            running = running + land[i].astype(F32)
 
     def reduce_finish(u, land, pre, tot, totland, reverse):
         wait_bytes(land.at[pl.ds(0, PLANE - 1)], rsem.at[u, 0])

time: 43 us -> 43 us (level)
  no operation moved by 1% of the time
where the time goes in v5:
time: 43 us; the launch traced here: 42.9 us
  Pallas kernels  42.2 us (98%)
  between operations  0.64 us (1%)
    pallas_call x1, Pallas kernels, local(): pl.pallas_call(functools.partial(kernel, factor), out_shape=(vm((tokens,...  41.1 us
    pallas_call x1, Pallas kernels, local(): pl.pallas_call(store, out_shape=(pltpu.HBM((tokens, width), BF16),) * 3,...  1.17 us

profile of v5, /device:TPU:1, one launch (start us, length us, event | category | flops | bytes accessed | tf_op | source)
XLA Modules:
  0.0 42.9 jit_solution(14327353344951126813)
XLA Ops:
  0.6 41.1 %shard_map.67 = (bf16[512,512]{1,0:T(8,128)(2,1)S(1)}, bf16[512,512]{1,0:T(8,128)(2,1)S(1)}, bf16[512,512]{1,0:T(8,128)(2,1)S(1)}) custom-call(bf16[512,512]{1,0:T(8,128)(2,1)} %q_hbm.1, bf16[512,512]{1,0:T(8,128)(2,1)} %k_hbm.1, bf16[512,512]{1,0:T(8,128)(2,1)} %v_hbm.1, bf16[64,4096]{1,0:T(8,128)(2,1)} %g_hbm.1), custom_call_target="tpu_custom_call" | custom-call | tf_op jit(solution)/shard_map/pallas_call | solution.py:315
  41.7 1.2 %shard_map.68 = (bf16[512,512]{1,0:T(8,128)(2,1)}, bf16[512,512]{1,0:T(8,128)(2,1)}, bf16[512,512]{1,0:T(8,128)(2,1)}) custom-call(bf16[512,512]{1,0:T(8,128)(2,1)S(1)} %get-tuple-element.6.qo_ref, bf16[512,512]{1,0:T(8,128)(2,1)S(1)} %get-tuple-element.7.ko_ref, bf16[512,512]{1,0:T(8,128)(2,1)S(1)} %get-tuple-element.8.vo_ref), custom_call_target="tpu_custom_call" | custom-call | tf_op jit(solution)/shard_map/pallas_call | solution.py:333
